TPU v7x, 32 devices: a whole 2x2x4 slice. The times are simulated.
32 devices in a mesh: inp: 4 (over z), wt: 4 (over y, x), out: 2 (over core).
Axes of the slice: x: 2, y: 2, z: 4, core: 2. Of those that a mesh axis runs over, the one named last changes fastest.
Arguments:
- tokens: bfloat16 [256, 16384], P(('wt', 'out'), 'inp'), may hold values from -6 to 6
- gate_weight: bfloat16 [16384, 26624], P('inp', ('wt', 'out')), may hold values from -0.046875 to 0.046875
- up_weight: bfloat16 [16384, 26624], P('inp', ('wt', 'out')), may hold values from -0.046875 to 0.046875
- hidden_grad: bfloat16 [256, 26624], P('inp', ('wt', 'out')), may hold values from -1.5 to 1.5
Outputs:
- input_grad: bfloat16 [256, 16384], P(('wt', 'out'), 'inp')
- gate_grad: bfloat16 [16384, 26624], P('inp', ('wt', 'out'))
- up_grad: bfloat16 [16384, 26624], P('inp', ('wt', 'out'))
All inputs are finite; a program needn't handle non-finite values.
Results may differ from a plain program's by a relative error of at most 0.0049.
Values may be sent and summed in bfloat16 or wider, within the bound.
A program may use at most 192 MiB of HBM per device.

v0:
```python
import jax
import jax.numpy as jnp
from jax import lax
from jax.sharding import PartitionSpec as P


def deltas(gate_act, up_act, grad):
    logistic = jax.nn.sigmoid(gate_act)
    up_delta = (grad * (gate_act * logistic)).astype(jnp.bfloat16)
    gate_delta = (grad * up_act * logistic * (1.0 + gate_act * (1.0 - logistic))).astype(
        jnp.bfloat16
    )
    return (gate_delta, up_delta)


def per_device(tokens, gate_weight, up_weight, hidden_grad):
    features = lax.all_gather(tokens, ("wt", "out"), axis=0, tiled=True)
    gate_act = jnp.dot(features, gate_weight, preferred_element_type=jnp.float32)
    up_act = jnp.dot(features, up_weight, preferred_element_type=jnp.float32)
    gate_act, up_act = lax.psum((gate_act, up_act), "inp")
    grad_all = lax.all_gather(hidden_grad, "inp", axis=0, tiled=True)
    gate_delta, up_delta = deltas(gate_act, up_act, grad_all.astype(jnp.float32))
    over_tokens = (((0,), (0,)), ((), ()))
    gate_grad = lax.dot_general(
        features, gate_delta, over_tokens, preferred_element_type=jnp.float32
    ).astype(jnp.bfloat16)
    up_grad = lax.dot_general(
        features, up_delta, over_tokens, preferred_element_type=jnp.float32
    ).astype(jnp.bfloat16)
    over_hidden = (((1,), (1,)), ((), ()))
    first = lax.dot_general(
        gate_delta, gate_weight, over_hidden, preferred_element_type=jnp.float32
    )
    summed = lax.psum_scatter(
        first
        + lax.dot_general(up_delta, up_weight, over_hidden, preferred_element_type=jnp.float32),
        ("wt", "out"),
        scatter_dimension=0,
        tiled=True,
    )
    return (summed.astype(jnp.bfloat16), gate_grad, up_grad)


def solution(mesh):
    return jax.shard_map(
        per_device,
        mesh=mesh,
        in_specs=(
            P(("wt", "out"), "inp"),
            P("inp", ("wt", "out")),
            P("inp", ("wt", "out")),
            P("inp", ("wt", "out")),
        ),
        out_specs=(P(("wt", "out"), "inp"), P("inp", ("wt", "out")), P("inp", ("wt", "out"))),
        check_vma=False,
    )
```

profile of v0, /device:TPU:0, one launch (start us, length us, event | category | flops | bytes accessed | tf_op | source)
XLA Modules:
  0.0 464.9 jit_solution(6898621832374541251)
XLA Ops:
  7.2 0.0 all-gather.5.cloned.1.call-start
  7.2 0.7 all-gather.5.cloned.1.call-update
  7.9 0.0 all-gather.3.cloned.1.call-start
  7.9 0.7 all-gather.3.cloned.1.call-update
  8.6 0.0 all-reduce.3.cloned.1.call-start
  8.7 31.8 %all-gather.5.cloned.1.call-done = bf16[256,4096]{1,0:T(8,128)(2,1)} async-done(((bf16[32,4096]{1,0:T(8,128)(2,1)}), bf16[256,4096]{1,0:T(8,128)(2,1)}) %all-gather.5.cloned.1.call-update) | async-done | bytes 2097168 | tf_op jit(solution)/shard_map/all_gather | solution.py:17
  40.5 0.0 copy-start
  40.5 18.5 %fusion.9 = f32[256,3328]{1,0:T(8,128)} fusion(bf16[256,4096]{1,0:T(8,128)(2,1)} %all-gather.5.cloned.1.call-done, bf16[4096,3328]{1,0:T(8,128)(2,1)} %param.5), kind=kOutput, calls=%fused_computation.13 | convolution fusion | flops 6979321856 | bytes 32768000 | tf_op jit(solution)/shard_map/dot_general | solution.py:18
  59.0 0.0 copy-done
  59.0 14.3 %fusion.8 = f32[256,3328]{1,0:T(8,128)} fusion(bf16[256,4096]{1,0:T(8,128)(2,1)S(1)} %copy-done, bf16[4096,3328]{1,0:T(8,128)(2,1)} %param.6), kind=kOutput, calls=%fused_computation.12 | convolution fusion | flops 6979321856 | bytes 32768000 | tf_op jit(solution)/shard_map/dot_general | solution.py:19
  73.4 0.0 all-reduce.3.cloned.1.call-update
  73.4 0.0 reduce-scatter.2.cloned.1.call-start
  73.4 7.9 %all-gather.3.cloned.1.call-done = bf16[256,3328]{1,0:T(8,128)(2,1)} async-done(((bf16[64,3328]{1,0:T(8,128)(2,1)}), bf16[256,3328]{1,0:T(8,128)(2,1)}) %all-gather.3.cloned.1.call-update) | async-done | bytes 1703952 | tf_op jit(solution)/shard_map/all_gather | solution.py:21
  81.4 242.0 %all-reduce.3.cloned.1.call-done = (f32[256,3328]{1,0:T(8,128)}, f32[256,3328]{1,0:T(8,128)}) async-done(((f32[256,3328]{1,0:T(8,128)}, f32[256,3328]{1,0:T(8,128)}), (f32[256,3328]{1,0:T(8,128)}, f32[256,3328]{1,0:T(8,128)})) %all-reduce.3.cloned.1.call-update) | async-done | bytes 6815760 | tf_op jit(solution)/shard_map/psum | solution.py:20
  323.4 4.8 %fusion.4 = bf16[256,3328]{1,0:T(8,128)(2,1)S(1)} fusion(f32[256,3328]{1,0:T(8,128)} %get-tuple-element.6, bf16[256,3328]{1,0:T(8,128)(2,1)} %all-gather.3.cloned.1.call-done, f32[256,3328]{1,0:T(8,128)} %get-tuple-element.7), kind=kLoop, calls=%fused_computation.9 | loop fusion | flops 9371648 | bytes 10223616 | tf_op jit(solution)/shard_map/convert_element_type | solution.py:10
  328.2 0.0 copy-start.1
  328.2 15.2 %fusion.10 = f32[256,4096]{1,0:T(8,128)} fusion(bf16[256,3328]{1,0:T(8,128)(2,1)S(1)} %fusion.4, bf16[4096,3328]{1,0:T(8,128)(2,1)} %param.5), kind=kOutput, calls=%fused_computation.14 | convolution fusion | flops 6979321856 | bytes 33161216 | tf_op jit(solution)/shard_map/dot_general | solution.py:31
  343.4 0.0 copy-done.1
  343.4 16.7 %convolution_add_fusion = f32[256,4096]{1,0:T(8,128)} fusion(f32[256,4096]{1,0:T(8,128)} %fusion.10, bf16[4096,3328]{1,0:T(8,128)(2,1)} %param.6, bf16[256,3328]{1,0:T(8,128)(2,1)S(1)} %copy-done.1, f32[256,3328]{1,0:T(8,128)} %get-tuple-element.7), kind=kOutput, calls=%fused_computation.4 | convolution fusion | flops 6986334208 | bytes 40763392 | tf_op jit(solution)/shard_map/dot_general | solution.py:36
  360.2 0.0 reduce-scatter.2.cloned.1.call-update
  360.2 15.5 %fusion.1 = bf16[4096,3328]{0,1:T(8,128)(2,1)} fusion(bf16[256,4096]{1,0:T(8,128)(2,1)} %all-gather.5.cloned.1.call-done, bf16[256,3328]{1,0:T(8,128)(2,1)S(1)} %copy-done.1, f32[256,3328]{1,0:T(8,128)} %get-tuple-element.7), kind=kOutput, calls=%fused_computation.3 | convolution fusion | flops 6998917120 | bytes 34471936 | tf_op jit(solution)/shard_map/dot_general | solution.py:27
  375.7 33.3 %copy.8 = bf16[4096,3328]{1,0:T(8,128)(2,1)} copy(bf16[4096,3328]{0,1:T(8,128)(2,1)} %fusion.1) | data formatting | bytes 54525952
  409.0 14.3 %fusion = bf16[4096,3328]{0,1:T(8,128)(2,1)} fusion(bf16[256,3328]{1,0:T(8,128)(2,1)S(1)} %fusion.4, bf16[256,4096]{1,0:T(8,128)(2,1)} %all-gather.5.cloned.1.call-done), kind=kOutput, calls=%fused_computation.2 | convolution fusion | flops 6992953344 | bytes 31064064 | tf_op jit(solution)/shard_map/dot_general | solution.py:24
  423.4 33.2 %copy.7 = bf16[4096,3328]{1,0:T(8,128)(2,1)} copy(bf16[4096,3328]{0,1:T(8,128)(2,1)} %fusion) | data formatting | bytes 54525952
  456.6 0.0 reduce-scatter.2.cloned.1.call-done
  456.6 1.8 convert_element_type.27
Async XLA Ops:
  7.2 33.4 %all-gather.5.cloned.1.call-start = ((), (), s32[]{:S(2)}) async-start(), calls=%async_computation.2 | async-start | bytes 2359296 | tf_op jit(solution)/shard_map/all_gather | solution.py:17
  7.9 73.5 %all-gather.3.cloned.1.call-start = ((), (), s32[]{:S(2)}) async-start(), calls=%async_computation.1 | async-start | bytes 2129920 | tf_op jit(solution)/shard_map/all_gather | solution.py:21
  8.6 314.7 %all-reduce.3.cloned.1.call-start = ((), (), s32[]{:S(2)}) async-start(), calls=%async_computation.4 | async-start | bytes 13631488 | tf_op jit(solution)/shard_map/psum | solution.py:20
  40.5 18.5 %copy-start = (bf16[256,4096]{1,0:T(8,128)(2,1)S(1)}, bf16[256,4096]{1,0:T(8,128)(2,1)}, u32[]{:S(2)}) copy-start(bf16[256,4096]{1,0:T(8,128)(2,1)} %all-gather.5.cloned.1.call-done) | copy-start | bytes 6291460
  73.4 383.2 %reduce-scatter.2.cloned.1.call-start = ((), (), s32[]{:S(2)}) async-start(), calls=%async_computation.3 | async-start | bytes 4718592 | tf_op jit(solution)/shard_map/reduce_scatter | solution.py:34
  328.2 15.2 %copy-start.1 = (bf16[256,3328]{1,0:T(8,128)(2,1)S(1)}, bf16[256,3328]{1,0:T(8,128)(2,1)}, u32[]{:S(2)}) copy-start(bf16[256,3328]{1,0:T(8,128)(2,1)} %all-gather.3.cloned.1.call-done) | copy-start | bytes 5111812
Sparse Core Ops, SparseCore 0:
  9.9 30.5 all-gather.4
  42.1 39.2 all-gather.2
  84.3 238.9 all-reduce.2
  360.3 50.2 reduce-scatter.1
where the time goes:
time: 467 us; the launch traced here: 465 us
  waiting for transfers between devices  283 us (61%)
  matrix products  94.6 us (20%)
  local copies, waits for them, and re-layouts  66.5 us (14%)
  between operations  13.8 us (3%)
  other arithmetic  6.59 us (1%)
    psum x1, waiting for transfers between devices, per_device(): gate_act, up_act = lax.psum((gate_act, up_act), 'inp')  242 us
    unnamed x6, local copies, waits for them, and re-layouts  66.5 us
    all_gather x1, waiting for transfers between devices, per_device(): features = lax.all_gather(tokens, ('wt', 'out'), axis=0, tiled=True)  31.8 us
    dot_general x1, matrix products, per_device(): jnp.dot(features, gate_weight, preferred_element_type=jnp.float32)  18.5 us
    dot_general x1, matrix products, per_device(): lax.dot_general(up_delta, up_weight, over_hidden, preferred_element_type=...  16.7 us
    dot_general x1, matrix products, per_device(): lax.dot_general(features, up_delta, over_tokens, preferred_element_type=j...  15.5 us
    dot_general x1, matrix products, per_device(): lax.dot_general(gate_delta, gate_weight, over_hidden, preferred_element_t...  15.2 us
    dot_general x1, matrix products, per_device(): up_act = jnp.dot(features, up_weight, preferred_element_type=jnp.float32)  14.3 us
  transfers between devices with their start and end apart: 4, of which 3 were waited for; matrix products, arithmetic and copies ran while one was open for 28% of the time, Pallas kernels for 0%

commit v1 on v0

v1 whole, which is shorter than its diff:
```python
import jax
import jax.numpy as jnp
from jax import lax
from jax.experimental import pallas as pl
from jax.experimental.pallas import tpu as pltpu
from jax.sharding import PartitionSpec as P

OVER_TOKENS = (((0,), (0,)), ((), ()))
OVER_HIDDEN = (((1,), (1,)), ((), ()))


def deltas(gate_act, up_act, grad):
    logistic = jax.nn.sigmoid(gate_act)
    up_delta = (grad * (gate_act * logistic)).astype(jnp.bfloat16)
    gate_delta = (grad * up_act * logistic * (1.0 + gate_act * (1.0 - logistic))).astype(
        jnp.bfloat16
    )
    return (gate_delta, up_delta)


def grads_kernel(features, gate_delta, up_delta, gate_grad, up_grad):
    for delta, grad in ((gate_delta, gate_grad), (up_delta, up_grad)):
        grad[...] = lax.dot_general(
            features[...], delta[...], OVER_TOKENS, preferred_element_type=jnp.float32
        ).astype(jnp.bfloat16)


def weight_grads(features, gate_delta, up_delta):
    tokens, width = features.shape
    hidden = gate_delta.shape[1]
    rows = 256
    grad = jax.ShapeDtypeStruct((width, hidden), jnp.bfloat16)
    return pl.pallas_call(
        grads_kernel,
        grid=(width // rows,),
        in_specs=[
            pl.BlockSpec((tokens, rows), lambda i: (0, i)),
            pl.BlockSpec((tokens, hidden), lambda i: (0, 0)),
            pl.BlockSpec((tokens, hidden), lambda i: (0, 0)),
        ],
        out_specs=[pl.BlockSpec((rows, hidden), lambda i: (i, 0))] * 2,
        out_shape=[grad, grad],
        compiler_params=pltpu.CompilerParams(vmem_limit_bytes=40 * 2**20),
        cost_estimate=pl.CostEstimate(
            flops=4 * tokens * width * hidden,
            bytes_accessed=4 * width * hidden,
            transcendentals=0,
        ),
    )(features, gate_delta, up_delta)


def per_device(tokens, gate_weight, up_weight, hidden_grad):
    features = lax.all_gather(tokens, ("wt", "out"), axis=0, tiled=True)
    gate_act = jnp.dot(features, gate_weight, preferred_element_type=jnp.float32)
    up_act = jnp.dot(features, up_weight, preferred_element_type=jnp.float32)
    gate_act, up_act = lax.psum_scatter(
        (gate_act, up_act), "inp", scatter_dimension=0, tiled=True
    )
    gate_delta, up_delta = deltas(gate_act, up_act, hidden_grad.astype(jnp.float32))
    gate_delta, up_delta = lax.all_gather((gate_delta, up_delta), "inp", axis=0, tiled=True)
    first = lax.dot_general(
        gate_delta, gate_weight, OVER_HIDDEN, preferred_element_type=jnp.float32
    )
    summed = lax.psum_scatter(
        first
        + lax.dot_general(up_delta, up_weight, OVER_HIDDEN, preferred_element_type=jnp.float32),
        ("wt", "out"),
        scatter_dimension=0,
        tiled=True,
    )
    gate_grad, up_grad = weight_grads(features, gate_delta, up_delta)
    return (summed.astype(jnp.bfloat16), gate_grad, up_grad)


def solution(mesh):
    return jax.shard_map(
        per_device,
        mesh=mesh,
        in_specs=(
            P(("wt", "out"), "inp"),
            P("inp", ("wt", "out")),
            P("inp", ("wt", "out")),
            P("inp", ("wt", "out")),
        ),
        out_specs=(P(("wt", "out"), "inp"), P("inp", ("wt", "out")), P("inp", ("wt", "out"))),
        check_vma=False,
    )
```

time: 467 us -> 349 us (0.75)
  local copies, waits for them, and re-layouts: 66.5 us -> 2.91 us
  waiting for transfers between devices: 283 us -> 242 us
  matrix products: 94.6 us -> 64 us
  Pallas kernels: 0 us -> 20.9 us
    psum x1 -> x0, waiting for transfers between devices: 242 us -> none  [per_device(): gate_act, up_act = lax.psum((gate_act, up_act), 'inp')]
    reduce_scatter x1 -> x3, waiting for transfers between devices: 0.01 us -> 144 us  [the longest x2 117 us: per_device(): lax.psum_scatter((gate_act, up_act), 'inp', scatter_dimension=0, tiled=True)]
    unnamed x6 -> x8, local copies, waits for them, and re-layouts: 66.5 us -> 2.91 us
    all_gather x1 -> x2, waiting for transfers between devices: 7.93 us -> 64.3 us  [per_device(): lax.all_gather((gate_delta, up_delta), 'inp', axis=0, tiled=True)]
    dot_general x4 -> x2, matrix products: 61.8 us -> 30.7 us  [the longest x1 16.1 us: per_device(): lax.dot_general(up_delta, up_weight, OVER_HIDDEN, preferred_element_type=...]
    pallas_call x0 -> x1, Pallas kernels: none -> 20.9 us  [weight_grads(): pl.pallas_call(grads_kernel, grid=(width // rows,), in_specs=[pl.BlockSpe...]
  transfers between devices with their start and end apart: 4 -> 6, of which waited for: 3 -> 6; matrix products, arithmetic and copies ran while one was open for 28% -> 8% of each run, Pallas kernels for 0% -> 6%
where the time goes in v1:
time: 349 us
  waiting for transfers between devices  242 us (69%)
  matrix products  64 us (18%)
  Pallas kernels  20.9 us (6%)
  between operations  14.1 us (4%)
  other arithmetic  4.49 us (1%)
    reduce_scatter x2, waiting for transfers between devices, per_device(): lax.psum_scatter((gate_act, up_act), 'inp', scatter_dimension=0, tiled=True)  117 us
    all_gather x2, waiting for transfers between devices, per_device(): lax.all_gather((gate_delta, up_delta), 'inp', axis=0, tiled=True)  64.3 us
    all_gather x1, waiting for transfers between devices, per_device(): features = lax.all_gather(tokens, ('wt', 'out'), axis=0, tiled=True)  32.6 us
    reduce_scatter x1, waiting for transfers between devices, per_device(): lax.psum_scatter(first + lax.dot_general(up_delta, up_weight, OVER_HIDDEN...  26.7 us
    pallas_call x1, Pallas kernels, weight_grads(): pl.pallas_call(grads_kernel, grid=(width // rows,), in_specs=[pl.BlockSpe...  20.9 us
    dot_general x1, matrix products, per_device(): jnp.dot(features, gate_weight, preferred_element_type=jnp.float32)  18.4 us
    dot_general x1, matrix products, per_device(): lax.dot_general(up_delta, up_weight, OVER_HIDDEN, preferred_element_type=...  16.1 us
    dot_general x1, matrix products, per_device(): up_act = jnp.dot(features, up_weight, preferred_element_type=jnp.float32)  14.9 us
  transfers between devices with their start and end apart: 6, of which 6 were waited for; matrix products, arithmetic and copies ran while one was open for 8% of the time, Pallas kernels for 6%

profile of v1, /device:TPU:0, one launch (start us, length us, event | category | flops | bytes accessed | tf_op | source)
XLA Modules:
  0.0 348.6 jit_solution(3797547292921621229)
XLA Ops:
  7.2 0.0 all-gather.4.cloned.1.call-start
  7.2 0.7 all-gather.4.cloned.1.call-update
  7.9 0.0 reduce-scatter.6.cloned.1.call-start
  7.9 32.6 %all-gather.4.cloned.1.call-done.features = bf16[256,4096]{1,0:T(8,128)(2,1)} async-done(((bf16[32,4096]{1,0:T(8,128)(2,1)}), bf16[256,4096]{1,0:T(8,128)(2,1)}) %all-gather.4.cloned.1.call-update) | async-done | bytes 2097168 | tf_op jit(solution)/shard_map/all_gather | solution.py:53
  40.5 0.0 copy-start
  40.5 18.4 %fusion.5 = f32[256,3328]{1,0:T(8,128)} fusion(bf16[256,4096]{1,0:T(8,128)(2,1)} %all-gather.4.cloned.1.call-done.features, bf16[4096,3328]{1,0:T(8,128)(2,1)} %param.5), kind=kOutput, calls=%fused_computation.9 | convolution fusion | flops 6979321856 | bytes 32768000 | tf_op jit(solution)/shard_map/dot_general | solution.py:54
  58.9 0.0 reduce-scatter.6.cloned.1.call-update
  59.0 0.0 copy-start.3
  59.0 0.0 reduce-scatter.4.cloned.1.call-start
  59.0 0.0 copy-done
  59.0 14.9 %fusion.4 = f32[256,3328]{1,0:T(8,128)} fusion(bf16[256,4096]{1,0:T(8,128)(2,1)S(1)} %copy-done, bf16[4096,3328]{1,0:T(8,128)(2,1)} %param.6), kind=kOutput, calls=%fused_computation.8 | convolution fusion | flops 6979321856 | bytes 32768000 | tf_op jit(solution)/shard_map/dot_general | solution.py:55
  73.9 0.0 reduce-scatter.4.cloned.1.call-update
  73.9 0.0 all-gather.6.cloned.1.call-start
  74.0 49.5 %reduce-scatter.6.cloned.1.call-done = f32[64,3328]{1,0:T(8,128)} async-done(((f32[256,3328]{1,0:T(8,128)}), f32[64,3328]{1,0:T(8,128)}) %reduce-scatter.6.cloned.1.call-update) | async-done | bytes 851984 | tf_op jit(solution)/shard_map/reduce_scatter | solution.py:56
  123.4 67.5 %reduce-scatter.4.cloned.1.call-done = f32[64,3328]{1,0:T(8,128)} async-done(((f32[256,3328]{1,0:T(8,128)}), f32[64,3328]{1,0:T(8,128)}) %reduce-scatter.4.cloned.1.call-update) | async-done | bytes 851984 | tf_op jit(solution)/shard_map/reduce_scatter | solution.py:56
  190.9 0.0 copy-done.3
  190.9 2.7 fusion.3
  193.6 0.0 all-gather.6.cloned.1.call-update
  193.7 0.0 all-gather.8.cloned.1.call-start
  193.7 0.5 all-gather.8.cloned.1.call-update
  194.2 0.2 reduce-scatter.8.cloned.1.call-start
  194.5 38.8 %all-gather.6.cloned.1.call-done.gate_delta = bf16[256,3328]{1,0:T(8,128)(2,1)} async-done(((bf16[64,3328]{1,0:T(8,128)(2,1)}), bf16[256,3328]{1,0:T(8,128)(2,1)}) %all-gather.6.cloned.1.call-update) | async-done | bytes 1703952 | tf_op jit(solution)/shard_map/all_gather | solution.py:60
  233.2 14.6 %fusion.6 = f32[256,4096]{1,0:T(8,128)} fusion(bf16[256,3328]{1,0:T(8,128)(2,1)} %all-gather.6.cloned.1.call-done.gate_delta, bf16[4096,3328]{1,0:T(8,128)(2,1)} %param.5), kind=kOutput, calls=%fused_computation.10 | convolution fusion | flops 6979321856 | bytes 33161216 | tf_op jit(solution)/shard_map/dot_general | solution.py:61
  247.8 25.5 %all-gather.8.cloned.1.call-done.up_delta = bf16[256,3328]{1,0:T(8,128)(2,1)} async-done(((bf16[64,3328]{1,0:T(8,128)(2,1)}), bf16[256,3328]{1,0:T(8,128)(2,1)}) %all-gather.8.cloned.1.call-update) | async-done | bytes 1703952 | tf_op jit(solution)/shard_map/all_gather | solution.py:60
  273.4 16.1 %convolution_add_fusion = f32[256,4096]{1,0:T(8,128)} fusion(f32[256,4096]{1,0:T(8,128)} %fusion.6, bf16[256,3328]{1,0:T(8,128)(2,1)} %all-gather.8.cloned.1.call-done.up_delta, bf16[4096,3328]{1,0:T(8,128)(2,1)} %param.6), kind=kOutput, calls=%fused_computation | convolution fusion | flops 6980370432 | bytes 37355520 | tf_op jit(solution)/shard_map/dot_general | solution.py:66
  289.5 0.0 reduce-scatter.8.cloned.1.call-update
  289.5 0.0 copy-start.1
  289.5 1.4 copy-done.1
  291.0 0.0 copy-start.2
  291.0 1.5 copy-done.2
  292.4 20.9 %shard_map.67 = (bf16[4096,3328]{1,0:T(8,128)(2,1)}, bf16[4096,3328]{1,0:T(8,128)(2,1)}) custom-call(bf16[256,4096]{1,0:T(8,128)(2,1)S(1)} %copy-done, bf16[256,3328]{1,0:T(8,128)(2,1)S(1)} %copy-done.1, bf16[256,3328]{1,0:T(8,128)(2,1)S(1)} %copy-done.2), custom_call_target="tpu_custom_call" | custom-call | flops 13958643712 | bytes 54525952 | tf_op jit(solution)/shard_map/pallas_call | solution.py:33
  313.3 26.7 %reduce-scatter.8.cloned.1.call-done = f32[32,4096]{1,0:T(8,128)} async-done(((f32[256,4096]{1,0:T(8,128)}), f32[32,4096]{1,0:T(8,128)}) %reduce-scatter.8.cloned.1.call-update) | async-done | bytes 524304 | tf_op jit(solution)/shard_map/reduce_scatter | solution.py:64
  340.0 1.8 convert_element_type.15
Async XLA Ops:
  7.2 33.4 %all-gather.4.cloned.1.call-start = ((), (), s32[]{:S(2)}) async-start(), calls=%async_computation.3 | async-start | bytes 2359296 | tf_op jit(solution)/shard_map/all_gather | solution.py:53
  7.9 115.5 %reduce-scatter.6.cloned.1.call-start = ((), (), s32[]{:S(2)}) async-start(), calls=%async_computation.5 | async-start | bytes 4259840 | tf_op jit(solution)/shard_map/reduce_scatter | solution.py:56
  40.5 18.5 %copy-start = (bf16[256,4096]{1,0:T(8,128)(2,1)S(1)}, bf16[256,4096]{1,0:T(8,128)(2,1)}, u32[]{:S(2)}) copy-start(bf16[256,4096]{1,0:T(8,128)(2,1)} %all-gather.4.cloned.1.call-done.features) | copy-start | bytes 6291460
  59.0 131.9 %copy-start.3 = (bf16[64,3328]{1,0:T(8,128)(2,1)S(1)}, bf16[64,3328]{1,0:T(8,128)(2,1)}, u32[]{:S(2)}) copy-start(bf16[64,3328]{1,0:T(8,128)(2,1)} %param.7) | copy-start | bytes 1277956
  59.0 131.9 %reduce-scatter.4.cloned.1.call-start = ((), (), s32[]{:S(2)}) async-start(), calls=%async_computation.4 | async-start | bytes 4259840 | tf_op jit(solution)/shard_map/reduce_scatter | solution.py:56
  73.9 159.3 %all-gather.6.cloned.1.call-start = ((), (), s32[]{:S(2)}) async-start(), calls=%async_computation.6 | async-start | bytes 2129920 | tf_op jit(solution)/shard_map/all_gather | solution.py:60
  193.7 79.7 %all-gather.8.cloned.1.call-start = ((), (), s32[]{:S(2)}) async-start(), calls=%async_computation.7 | async-start | bytes 2129920 | tf_op jit(solution)/shard_map/all_gather | solution.py:60
  194.2 145.7 %reduce-scatter.8.cloned.1.call-start = ((), (), s32[]{:S(2)}) async-start(), calls=%async_computation.8 | async-start | bytes 4718592 | tf_op jit(solution)/shard_map/reduce_scatter | solution.py:64
  289.5 1.5 copy-start.1
  291.0 1.5 copy-start.2
Sparse Core Ops, SparseCore 0:
  9.9 30.5 all-gather.3
  59.1 64.3 reduce-scatter.5
  126.3 64.5 reduce-scatter.3
  193.8 39.4 all-gather.5
  235.2 38.0 all-gather.7
  289.6 50.2 reduce-scatter.7

commit v2 on v1

--- a/solution.py
+++ b/solution.py
@@ -1,3 +1,5 @@
+import functools
+
 import jax
 import jax.numpy as jnp
 from jax import lax
@@ -72,9 +74,377 @@
     return (summed.astype(jnp.bfloat16), gate_grad, up_grad)
 
 
+MESH = pl.DeviceIdType.MESH
+CHUNK = 256
+SUM_LAG, DELTA_LAG, MID_LAG, EDGE_LAG = 1, 3, 4, 6
+
+
+def exchange_kernel(
+    chunks,
+    tokens, hidden, gate_weight, up_weight,
+    input_grad, features_out, delta_out,
+    features, grads, forward_w, backward_w, acts_out, from_edge, from_mid, delta, own, total,
+    pair_in, plane_out, plane_in,
+    gather_send, gather_recv, relay_send, relay_recv, grad_send, grad_recv,
+    forward_sem, backward_sem, act_send, edge_recv, mid_recv, delta_send, delta_recv,
+    pair_send, pair_recv, plane_send, plane_recv, out_sem,
+):
+    z, wt, out = lax.axis_index("inp"), lax.axis_index("wt"), lax.axis_index("out")
+    rows, width = tokens.shape
+    chunk_rows = hidden.shape[0]
+    is_mid = jnp.logical_and(z > 0, z < 3)
+    is_edge = jnp.logical_not(is_mid)
+    paired = z + 1 - 2 * lax.rem(z, 2)
+    other_mid = 3 - z
+    plane = (None, wt + 1 - 2 * lax.rem(wt, 2), lax.rem(wt + 2, 4), 3 - wt)
+    core = {"out": 1 - out}
+
+    def remote(src, dst, send, recv, to):
+        return pltpu.make_async_remote_copy(
+            src_ref=src, dst_ref=dst, send_sem=send, recv_sem=recv,
+            device_id=to, device_id_type=MESH,
+        )
+
+    def weight_copies(c, slots, sems):
+        slot = lax.rem(c, 2)
+        columns = pl.ds(pl.multiple_of(c * CHUNK, CHUNK), CHUNK)
+        return [
+            pltpu.make_async_copy(
+                w.at[:, columns], slots.at[slot, :, pl.ds(i * CHUNK, CHUNK)], sems.at[slot, i]
+            )
+            for i, w in enumerate((gate_weight, up_weight))
+        ]
+
+    for c in range(2):
+        for copy in weight_copies(c, forward_w, forward_sem):
+            copy.start()
+        for copy in weight_copies(c, backward_w, backward_sem):
+            copy.start()
+
+    barrier = pltpu.get_barrier_semaphore()
+    for k in (1, 2, 3):
+        pl.semaphore_signal(barrier, inc=1, device_id={"wt": plane[k]}, device_id_type=MESH)
+    pl.semaphore_signal(barrier, inc=1, device_id=core, device_id_type=MESH)
+    pl.semaphore_signal(barrier, inc=1, device_id={"inp": paired}, device_id_type=MESH)
+
+    @pl.when(is_mid)
+    def _():
+        pl.semaphore_signal(barrier, inc=1, device_id={"inp": other_mid}, device_id_type=MESH)
+        pl.semaphore_wait(barrier, 6)
+
+    @pl.when(is_edge)
+    def _():
+        pl.semaphore_wait(barrier, 5)
+
+    def block(w, o):
+        return pl.ds(pl.multiple_of((w * 2 + o) * rows, rows), rows)
+
+    mine = block(wt, out)
+    gathers = [remote(tokens, features.at[mine], gather_send.at[0], gather_recv.at[0], core)]
+    for k in (3, 1, 2):
+        gathers.append(
+            remote(tokens, features.at[mine], gather_send.at[k], gather_recv.at[k], {"wt": plane[k]})
+        )
+    for copy in gathers:
+        copy.start()
+
+    @pl.when(is_edge)
+    def _():
+        remote(hidden, grads.at[z], grad_send.at[0], grad_recv.at[0], {"inp": paired}).start()
+
+    @pl.when(is_mid)
+    def _():
+        remote(hidden, grads.at[z], grad_send.at[0], grad_recv.at[1], {"inp": other_mid}).start()
+        grads[z] = hidden[...]
+
+    features[mine, :] = tokens[...]
+    total[...] = jnp.zeros_like(total)
+
+    relays = []
+    for k in (1, 2, 3):
+        theirs = block(plane[k], out)
+        remote(
+            tokens, features.at[theirs], gather_send.at[k], gather_recv.at[k], {"wt": plane[k]}
+        ).wait_recv()
+        relay = remote(
+            features.at[theirs], features.at[theirs], relay_send.at[k], relay_recv.at[k], core
+        )
+        relay.start()
+        relays.append(relay)
+
+    def relayed_grads():
+        return remote(
+            grads.at[paired], grads.at[paired], grad_send.at[1], grad_recv.at[2], {"inp": other_mid}
+        )
+
+    @pl.when(is_mid)
+    def _():
+        remote(
+            hidden, grads.at[paired], grad_send.at[0], grad_recv.at[0], {"inp": paired}
+        ).wait_recv()
+        relayed_grads().start()
+
+    remote(
+        tokens, features.at[block(wt, 1 - out)], gather_send.at[0], gather_recv.at[0], core
+    ).wait_recv()
+    for k in (1, 2, 3):
+        theirs = block(plane[k], 1 - out)
+        remote(
+            features.at[theirs], features.at[theirs], relay_send.at[k], relay_recv.at[k], core
+        ).wait_recv()
+    features_copy = pltpu.make_async_copy(features, features_out, out_sem.at[0])
+    features_copy.start()
+
+    def edge_copy(c):
+        return remote(
+            acts_out.at[c], from_edge.at[c], act_send.at[c], edge_recv.at[c], {"inp": paired}
+        )
+
+    def mid_copy(c):
+        return remote(
+            acts_out.at[c], from_mid.at[c], act_send.at[c], mid_recv.at[c], {"inp": other_mid}
+        )
+
+    def delta_copy(c):
+        return remote(
+            delta.at[c], delta.at[c], delta_send.at[c], delta_recv.at[c], {"inp": paired}
+        )
+
+    def step(t, carry):
+        @pl.when(t < chunks)
+        def _():
+            for copy in weight_copies(t, forward_w, forward_sem):
+                copy.wait()
+            partial = jnp.dot(
+                features[...], forward_w[lax.rem(t, 2)], preferred_element_type=jnp.float32
+            )
+
+            @pl.when(is_edge)
+            def _():
+                acts_out[t] = partial.astype(jnp.bfloat16)
+                edge_copy(t).start()
+
+            @pl.when(is_mid)
+            def _():
+                own[t] = partial
+
+            @pl.when(t + 2 < chunks)
+            def _():
+                for copy in weight_copies(t + 2, forward_w, forward_sem):
+                    copy.start()
+
+        c1 = t - SUM_LAG
+
+        @pl.when(is_mid & (c1 >= 0) & (c1 < chunks))
+        def _():
+            edge_copy(c1).wait_recv()
+            both = own[c1] + from_edge[c1].astype(jnp.float32)
+            own[c1] = both
+            acts_out[c1] = both.astype(jnp.bfloat16)
+            mid_copy(c1).start()
+
+        c2 = t - DELTA_LAG
+
+        @pl.when(is_mid & (c2 == 0))
+        def _():
+            remote(
+                hidden, grads.at[other_mid], grad_send.at[0], grad_recv.at[1], {"inp": other_mid}
+            ).wait_recv()
+            far = 3 - paired
+            remote(
+                grads.at[far], grads.at[far], grad_send.at[1], grad_recv.at[2], {"inp": other_mid}
+            ).wait_recv()
+
+        @pl.when(is_mid & (c2 >= 0) & (c2 < chunks))
+        def _():
+            mid_copy(c2).wait_recv()
+            columns = pl.ds(pl.multiple_of(c2 * CHUNK, CHUNK), CHUNK)
+            for q in range(4):
+                part = pl.ds(q * chunk_rows, chunk_rows)
+                acts = own[c2, part, :] + from_mid[c2, part, :].astype(jnp.float32)
+                gate_delta, up_delta = deltas(
+                    acts[:, :CHUNK], acts[:, CHUNK:], grads[q, :, columns].astype(jnp.float32)
+                )
+                delta[c2, part, pl.ds(0, CHUNK)] = gate_delta
+                delta[c2, part, pl.ds(CHUNK, CHUNK)] = up_delta
+            delta_copy(c2).start()
+
+        cb = t - jnp.where(is_mid, MID_LAG, EDGE_LAG)
+
+        @pl.when((cb >= 0) & (cb < chunks))
+        def _():
+            @pl.when(is_edge)
+            def _():
+                delta_copy(cb).wait_recv()
+
+            for copy in weight_copies(cb, backward_w, backward_sem):
+                copy.wait()
+            slot = lax.rem(cb, 2)
+
+            def piece(i, carry):
+                at = pl.ds(pl.multiple_of(i * 512, 512), 512)
+                total[:, at] += lax.dot_general(
+                    delta[cb], backward_w[slot, at, :], OVER_HIDDEN,
+                    preferred_element_type=jnp.float32,
+                )
+                return carry
+
+            lax.fori_loop(0, width // 512, piece, 0)
+
+            @pl.when(cb + 2 < chunks)
+            def _():
+                for copy in weight_copies(cb + 2, backward_w, backward_sem):
+                    copy.start()
+
+        return carry
+
+    lax.fori_loop(0, chunks + EDGE_LAG, step, 0)
+    delta_out_copy = pltpu.make_async_copy(delta, delta_out, out_sem.at[1])
+    delta_out_copy.start()
+
+    targets = (wt,) + plane[1:]
+
+    def pair_copy(k, o):
+        return remote(
+            total.at[block(targets[k], o)], pair_in.at[k], pair_send.at[k], pair_recv.at[k], core
+        )
+
+    for k in (3, 1, 2, 0):
+        pair_copy(k, 1 - out).start()
+    for k in (3, 1, 2):
+        pair_copy(k, 1 - out).wait_recv()
+        plane_out[k - 1] = (total[block(targets[k], out), :] + pair_in[k]).astype(jnp.bfloat16)
+        remote(
+            plane_out.at[k - 1], plane_in.at[k - 1], plane_send.at[k], plane_recv.at[k],
+            {"wt": plane[k]},
+        ).start()
+    pair_copy(0, 1 - out).wait_recv()
+    result = total[mine, :] + pair_in[0]
+    for k in (1, 2, 3):
+        copy = remote(
+            plane_out.at[k - 1], plane_in.at[k - 1], plane_send.at[k], plane_recv.at[k],
+            {"wt": plane[k]},
+        )
+        copy.wait_recv()
+        result = result + plane_in[k - 1].astype(jnp.float32)
+        copy.wait_send()
+    input_grad[...] = result.astype(jnp.bfloat16)
+
+    for k in range(4):
+        pair_copy(k, 1 - out).wait_send()
+    for copy in gathers + relays:
+        copy.wait_send()
+    remote(hidden, grads.at[z], grad_send.at[0], grad_recv.at[0], {"inp": paired}).wait_send()
+
+    @pl.when(is_mid)
+    def _():
+        relayed_grads().wait_send()
+
+    def finish(c, carry):
+        edge_copy(c).wait_send()
+
+        @pl.when(is_mid)
+        def _():
+            delta_copy(c).wait_send()
+
+        return carry
+
+    lax.fori_loop(0, chunks, finish, 0)
+    features_copy.wait()
+    delta_out_copy.wait()
+
+
+def exchange(tokens, gate_weight, up_weight, hidden_grad):
+    rows, width = tokens.shape
+    hidden = gate_weight.shape[1]
+    chunks = hidden // CHUNK
+    whole = rows * 8
+    bf16, f32 = jnp.bfloat16, jnp.float32
+    dma = pltpu.SemaphoreType.DMA
+    vmem, hbm = pl.BlockSpec(memory_space=pltpu.VMEM), pl.BlockSpec(memory_space=pl.ANY)
+    acts = (chunks, whole, 2 * CHUNK)
+    return pl.pallas_call(
+        functools.partial(exchange_kernel, chunks),
+        out_shape=(
+            jax.ShapeDtypeStruct((rows, width), bf16),
+            jax.ShapeDtypeStruct((whole, width), bf16),
+            jax.ShapeDtypeStruct(acts, bf16),
+        ),
+        in_specs=[vmem, vmem, hbm, hbm],
+        out_specs=(vmem, hbm, hbm),
+        scratch_shapes=[
+            pltpu.VMEM((whole, width), bf16),
+            pltpu.VMEM((4, whole // 4, hidden), bf16),
+            pltpu.VMEM((2, width, 2 * CHUNK), bf16),
+            pltpu.VMEM((2, width, 2 * CHUNK), bf16),
+            pltpu.VMEM(acts, bf16),
+            pltpu.VMEM(acts, bf16),
+            pltpu.VMEM(acts, bf16),
+            pltpu.VMEM(acts, bf16),
+            pltpu.VMEM(acts, f32),
+            pltpu.VMEM((whole, width), f32),
+            pltpu.VMEM((4, rows, width), f32),
+            pltpu.VMEM((3, rows, width), bf16),
+            pltpu.VMEM((3, rows, width), bf16),
+            dma((4,)), dma((4,)), dma((4,)), dma((4,)), dma((2,)), dma((3,)),
+            dma((2, 2)), dma((2, 2)),
+            dma((chunks,)), dma((chunks,)), dma((chunks,)), dma((chunks,)), dma((chunks,)),
+            dma((4,)), dma((4,)), dma((4,)), dma((4,)), dma((2,)),
+        ],
+        compiler_params=pltpu.CompilerParams(
+            collective_id=0, has_side_effects=True, vmem_limit_bytes=58 * 2**20
+        ),
+        cost_estimate=pl.CostEstimate(
+            flops=8 * whole * width * hidden,
+            bytes_accessed=8 * width * hidden,
+            transcendentals=whole * hidden,
+        ),
+    )(tokens, hidden_grad, gate_weight, up_weight)
+
+
+def chunk_grads_kernel(features, delta, gate_grad, up_grad):
+    turned = features[...].T
+    for c in range(delta.shape[0]):
+        both = jnp.dot(turned, delta[c], preferred_element_type=jnp.float32).astype(jnp.bfloat16)
+        at = pl.ds(c * CHUNK, CHUNK)
+        gate_grad[:, at] = both[:, :CHUNK]
+        up_grad[:, at] = both[:, CHUNK:]
+
+
+def chunk_grads(features, delta):
+    tokens, width = features.shape
+    chunks = delta.shape[0]
+    hidden = chunks * CHUNK
+    rows = 256
+    grad = jax.ShapeDtypeStruct((width, hidden), jnp.bfloat16)
+    return pl.pallas_call(
+        chunk_grads_kernel,
+        grid=(width // rows,),
+        in_specs=[
+            pl.BlockSpec((tokens, rows), lambda i: (0, i)),
+            pl.BlockSpec(delta.shape, lambda i: (0, 0, 0)),
+        ],
+        out_specs=[pl.BlockSpec((rows, hidden), lambda i: (i, 0))] * 2,
+        out_shape=[grad, grad],
+        compiler_params=pltpu.CompilerParams(vmem_limit_bytes=40 * 2**20),
+        cost_estimate=pl.CostEstimate(
+            flops=4 * tokens * width * hidden,
+            bytes_accessed=4 * width * hidden,
+            transcendentals=0,
+        ),
+    )(features, delta)
+
+
+def on_line(tokens, gate_weight, up_weight, hidden_grad):
+    input_grad, features, delta = exchange(tokens, gate_weight, up_weight, hidden_grad)
+    gate_grad, up_grad = chunk_grads(features, delta)
+    return (input_grad, gate_grad, up_grad)
+
+
 def solution(mesh):
+    line = (mesh.shape["inp"], mesh.shape["wt"], mesh.shape["out"]) == (4, 4, 2)
     return jax.shard_map(
-        per_device,
+        on_line if line else per_device,
         mesh=mesh,
         in_specs=(
             P(("wt", "out"), "inp"),

time: 349 us -> 164 us (0.47)
  waiting for transfers between devices: 242 us -> 0 us
  Pallas kernels: 20.9 us -> 159 us
  matrix products: 64 us -> 0 us
  between operations: 14.1 us -> 0.65 us
  other arithmetic: 4.49 us -> 0 us
    reduce_scatter x3 -> x0, waiting for transfers between devices: 144 us -> none  [the longest x2 117 us: per_device(): lax.psum_scatter((gate_act, up_act), 'inp', scatter_dimension=0, tiled=True)]
    pallas_call x1 -> x2, Pallas kernels: 20.9 us -> 159 us  [the longest x1 135 us: exchange(): pl.pallas_call(functools.partial(exchange_kernel, chunks), out_shape=(jax...]
    all_gather x3 -> x0, waiting for transfers between devices: 96.9 us -> none  [the longest x2 64.3 us: per_device(): lax.all_gather((gate_delta, up_delta), 'inp', axis=0, tiled=True)]
    dot_general x4 -> x0, matrix products: 64 us -> none  [the longest x1 18.4 us: per_device(): jnp.dot(features, gate_weight, preferred_element_type=jnp.float32)]
    convert_element_type x2 -> x0, other arithmetic: 4.49 us -> none  [the longest x1 2.72 us: deltas(): up_delta = (grad * (gate_act * logistic)).astype(jnp.bfloat16)]
  transfers between devices with their start and end apart: 6 -> 0, of which waited for: 6 -> 0; matrix products, arithmetic and copies ran while one was open for 8% -> 0% of each run, Pallas kernels for 6% -> 0%
where the time goes in v2:
time: 164 us; the launch traced here: 163 us
  Pallas kernels  159 us (97%)
  local copies, waits for them, and re-layouts  4.25 us (3%)
    pallas_call x1, Pallas kernels, exchange(): pl.pallas_call(functools.partial(exchange_kernel, chunks), out_shape=(jax...  135 us
    pallas_call x1, Pallas kernels, chunk_grads(): pl.pallas_call(chunk_grads_kernel, grid=(width // rows,), in_specs=[pl.Bl...  23.5 us
    unnamed x7, local copies, waits for them, and re-layouts  4.25 us

profile of v2, /device:TPU:0, one launch (start us, length us, event | category | flops | bytes accessed | tf_op | source)
XLA Modules:
  0.0 163.4 jit_solution(12070440531825368493)
XLA Ops:
  0.6 135.0 %shard_map.67 = (bf16[32,4096]{1,0:T(8,128)(2,1)}, bf16[256,4096]{1,0:T(8,128)(2,1)}, bf16[13,256,512]{2,1,0:T(8,128)(2,1)}) custom-call(bf16[32,4096]{1,0:T(8,128)(2,1)} %tokens.1, bf16[64,3328]{1,0:T(8,128)(2,1)} %hidden.1, bf16[4096,3328]{1,0:T(8,128)(2,1)} %gate_weight.1, bf16[4096,3328]{1,0:T(8,128)(2,1)} %up_weight.1), custom_call_target="tpu_custom_call" | custom-call | flops 27917287424 | bytes 109051904 | tf_op jit(solution)/shard_map/pallas_call | solution.py:366
  135.7 0.0 copy-start
  135.7 2.0 %copy-done = bf16[13,256,512]{2,1,0:T(8,128)(2,1)S(1)} copy-done((bf16[13,256,512]{2,1,0:T(8,128)(2,1)S(1)}, bf16[13,256,512]{2,1,0:T(8,128)(2,1)}, u32[]{:S(2)}) %copy-start) | copy-done | bytes 3407896
  137.6 0.0 copy-start.1
  137.6 1.6 copy-done.1
  139.2 0.0 copy-start.2
  139.2 23.5 %shard_map.68 = (bf16[4096,3328]{1,0:T(8,128)(2,1)}, bf16[4096,3328]{1,0:T(8,128)(2,1)}) custom-call(bf16[256,4096]{1,0:T(8,128)(2,1)S(1)} %copy-done.1, bf16[13,256,512]{2,1,0:T(8,128)(2,1)S(1)} %copy-done), custom_call_target="tpu_custom_call" | custom-call | flops 13958643712 | bytes 54525952 | tf_op jit(solution)/shard_map/pallas_call | solution.py:420
  162.7 0.0 copy-done.2
  162.7 0.7 copy.8
Async XLA Ops:
  135.7 2.0 %copy-start = (bf16[13,256,512]{2,1,0:T(8,128)(2,1)S(1)}, bf16[13,256,512]{2,1,0:T(8,128)(2,1)}, u32[]{:S(2)}) copy-start(bf16[13,256,512]{2,1,0:T(8,128)(2,1)} %get-tuple-element.10.delta) | copy-start | bytes 10223620
  137.6 1.6 copy-start.1
  139.2 23.5 %copy-start.2 = (bf16[32,4096]{1,0:T(8,128)(2,1)S(1)}, bf16[32,4096]{1,0:T(8,128)(2,1)}, u32[]{:S(2)}) copy-start(bf16[32,4096]{1,0:T(8,128)(2,1)} %get-tuple-element.16) | copy-start | bytes 786436

commit v3 on v2

--- a/solution.py
+++ b/solution.py
@@ -76,7 +76,7 @@
 
 MESH = pl.DeviceIdType.MESH
 CHUNK = 256
-SUM_LAG, DELTA_LAG, MID_LAG, EDGE_LAG = 1, 3, 4, 6
+SUM_LAG, DELTA_LAG, MID_LAG, EDGE_LAG = 1, 2, 3, 8
 
 
 def exchange_kernel(
@@ -243,6 +243,33 @@
             acts_out[c1] = both.astype(jnp.bfloat16)
             mid_copy(c1).start()
 
+        cb = t - jnp.where(is_mid, MID_LAG, EDGE_LAG)
+
+        @pl.when((cb >= 0) & (cb < chunks))
+        def _():
+            @pl.when(is_edge)
+            def _():
+                delta_copy(cb).wait_recv()
+
+            for copy in weight_copies(cb, backward_w, backward_sem):
+                copy.wait()
+            slot = lax.rem(cb, 2)
+
+            def piece(i, carry):
+                at = pl.ds(pl.multiple_of(i * 512, 512), 512)
+                total[:, at] += lax.dot_general(
+                    delta[cb], backward_w[slot, at, :], OVER_HIDDEN,
+                    preferred_element_type=jnp.float32,
+                )
+                return carry
+
+            lax.fori_loop(0, width // 512, piece, 0)
+
+            @pl.when(cb + 2 < chunks)
+            def _():
+                for copy in weight_copies(cb + 2, backward_w, backward_sem):
+                    copy.start()
+
         c2 = t - DELTA_LAG
 
         @pl.when(is_mid & (c2 == 0))
@@ -268,33 +295,6 @@
                 delta[c2, part, pl.ds(0, CHUNK)] = gate_delta
                 delta[c2, part, pl.ds(CHUNK, CHUNK)] = up_delta
             delta_copy(c2).start()
-
-        cb = t - jnp.where(is_mid, MID_LAG, EDGE_LAG)
-
-        @pl.when((cb >= 0) & (cb < chunks))
-        def _():
-            @pl.when(is_edge)
-            def _():
-                delta_copy(cb).wait_recv()
-
-            for copy in weight_copies(cb, backward_w, backward_sem):
-                copy.wait()
-            slot = lax.rem(cb, 2)
-
-            def piece(i, carry):
-                at = pl.ds(pl.multiple_of(i * 512, 512), 512)
-                total[:, at] += lax.dot_general(
-                    delta[cb], backward_w[slot, at, :], OVER_HIDDEN,
-                    preferred_element_type=jnp.float32,
-                )
-                return carry
-
-            lax.fori_loop(0, width // 512, piece, 0)
-
-            @pl.when(cb + 2 < chunks)
-            def _():
-                for copy in weight_copies(cb + 2, backward_w, backward_sem):
-                    copy.start()
 
         return carry
 
@@ -402,13 +402,15 @@
     )(tokens, hidden_grad, gate_weight, up_weight)
 
 
-def chunk_grads_kernel(features, delta, gate_grad, up_grad):
-    turned = features[...].T
-    for c in range(delta.shape[0]):
-        both = jnp.dot(turned, delta[c], preferred_element_type=jnp.float32).astype(jnp.bfloat16)
-        at = pl.ds(c * CHUNK, CHUNK)
-        gate_grad[:, at] = both[:, :CHUNK]
-        up_grad[:, at] = both[:, CHUNK:]
+def chunk_grads_kernel(features, delta, gate_grad, up_grad, gate_delta, up_delta):
+    @pl.when(pl.program_id(0) == 0)
+    def _():
+        for c in range(delta.shape[0]):
+            at = pl.ds(c * CHUNK, CHUNK)
+            gate_delta[:, at] = delta[c, :, pl.ds(0, CHUNK)]
+            up_delta[:, at] = delta[c, :, pl.ds(CHUNK, CHUNK)]
+
+    grads_kernel(features, gate_delta, up_delta, gate_grad, up_grad)
 
 
 def chunk_grads(features, delta):
@@ -426,6 +428,7 @@
         ],
         out_specs=[pl.BlockSpec((rows, hidden), lambda i: (i, 0))] * 2,
         out_shape=[grad, grad],
+        scratch_shapes=[pltpu.VMEM((tokens, hidden), jnp.bfloat16)] * 2,
         compiler_params=pltpu.CompilerParams(vmem_limit_bytes=40 * 2**20),
         cost_estimate=pl.CostEstimate(
             flops=4 * tokens * width * hidden,

time: 164 us -> 158 us (0.963)
  Pallas kernels: 159 us -> 153 us
    pallas_call x1, Pallas kernels: 23.5 us -> 20.5 us  [chunk_grads(): pl.pallas_call(chunk_grads_kernel, grid=(width // rows,), in_specs=[pl.Bl...]
    pallas_call x1, Pallas kernels: 135 us -> 132 us  [exchange(): pl.pallas_call(functools.partial(exchange_kernel, chunks), out_shape=(jax...]
where the time goes in v3:
time: 158 us; the launch traced here: 157 us
  Pallas kernels  153 us (97%)
  local copies, waits for them, and re-layouts  4.25 us (3%)
    pallas_call x1, Pallas kernels, exchange(): pl.pallas_call(functools.partial(exchange_kernel, chunks), out_shape=(jax...  132 us
    pallas_call x1, Pallas kernels, chunk_grads(): pl.pallas_call(chunk_grads_kernel, grid=(width // rows,), in_specs=[pl.Bl...  20.5 us
    unnamed x7, local copies, waits for them, and re-layouts  4.25 us

profile of v3, /device:TPU:0, one launch (start us, length us, event | category | flops | bytes accessed | tf_op | source)
XLA Modules:
  0.0 157.5 jit_solution(9959235309108473237)
XLA Ops:
  0.6 132.1 %shard_map.67 = (bf16[32,4096]{1,0:T(8,128)(2,1)}, bf16[256,4096]{1,0:T(8,128)(2,1)}, bf16[13,256,512]{2,1,0:T(8,128)(2,1)}) custom-call(bf16[32,4096]{1,0:T(8,128)(2,1)} %tokens.1, bf16[64,3328]{1,0:T(8,128)(2,1)} %hidden.1, bf16[4096,3328]{1,0:T(8,128)(2,1)} %gate_weight.1, bf16[4096,3328]{1,0:T(8,128)(2,1)} %up_weight.1), custom_call_target="tpu_custom_call" | custom-call | flops 27917287424 | bytes 109051904 | tf_op jit(solution)/shard_map/pallas_call | solution.py:366
  132.8 0.0 copy-start
  132.8 2.0 %copy-done = bf16[13,256,512]{2,1,0:T(8,128)(2,1)S(1)} copy-done((bf16[13,256,512]{2,1,0:T(8,128)(2,1)S(1)}, bf16[13,256,512]{2,1,0:T(8,128)(2,1)}, u32[]{:S(2)}) %copy-start) | copy-done | bytes 3407896
  134.7 0.0 copy-start.1
  134.7 1.6 %copy-done.1 = bf16[256,4096]{1,0:T(8,128)(2,1)S(1)} copy-done((bf16[256,4096]{1,0:T(8,128)(2,1)S(1)}, bf16[256,4096]{1,0:T(8,128)(2,1)}, u32[]{:S(2)}) %copy-start.1) | copy-done | bytes 2097176
  136.3 0.0 copy-start.2
  136.3 20.5 %shard_map.68 = (bf16[4096,3328]{1,0:T(8,128)(2,1)}, bf16[4096,3328]{1,0:T(8,128)(2,1)}) custom-call(bf16[256,4096]{1,0:T(8,128)(2,1)S(1)} %copy-done.1, bf16[13,256,512]{2,1,0:T(8,128)(2,1)S(1)} %copy-done), custom_call_target="tpu_custom_call" | custom-call | flops 13958643712 | bytes 54525952 | tf_op jit(solution)/shard_map/pallas_call | solution.py:422
  156.8 0.0 copy-done.2
  156.8 0.7 copy.8
Async XLA Ops:
  132.8 2.0 %copy-start = (bf16[13,256,512]{2,1,0:T(8,128)(2,1)S(1)}, bf16[13,256,512]{2,1,0:T(8,128)(2,1)}, u32[]{:S(2)}) copy-start(bf16[13,256,512]{2,1,0:T(8,128)(2,1)} %get-tuple-element.10.delta) | copy-start | bytes 10223620
  134.7 1.6 %copy-start.1 = (bf16[256,4096]{1,0:T(8,128)(2,1)S(1)}, bf16[256,4096]{1,0:T(8,128)(2,1)}, u32[]{:S(2)}) copy-start(bf16[256,4096]{1,0:T(8,128)(2,1)} %get-tuple-element.9.features) | copy-start | bytes 6291460
  136.3 20.5 %copy-start.2 = (bf16[32,4096]{1,0:T(8,128)(2,1)S(1)}, bf16[32,4096]{1,0:T(8,128)(2,1)}, u32[]{:S(2)}) copy-start(bf16[32,4096]{1,0:T(8,128)(2,1)} %get-tuple-element.16) | copy-start | bytes 786436
